TPU v7x, 128 devices: a whole 4x4x4 slice. The times are simulated.
128 devices in a mesh: lon: 16 (over x, z), lat: 2 (over y_lo), mem: 4 (over y_hi, core).
Axes of the slice: x: 4, y: 4 (y_hi: 2, y_lo: 2; y = y_hi * 2 + y_lo), z: 4, core: 2. Of those that a mesh axis runs over, the one named last changes fastest.
Arguments:
- perturb: float32 [8, 2, 2048, 4096], P('mem', None, 'lat', 'lon'), may hold values from -6 to 6
- control: float32 [8, 2, 2048, 4096], P('mem', None, 'lat', 'lon'), may hold values from -6 to 6
- diffusivity: float32 [2048, 4096], P('lat', 'lon'), may hold values from 0.05 to 0.24
- sea_mask: int32 [2, 2048, 4096], P(None, 'lat', 'lon'), may hold values 0 or 1
- fold_partner: int32 [4096], replicated, may hold values from 0 to 4095, as said below
Outputs:
- increment: float32 [2, 2048, 4096], P(None, 'lat', 'lon')
Inputs may be any that keep to these rules, and one draw needn't show every extreme that they name: `sea_mask`: 1 marks sea and 0 land. fold_partner[i] = (2 p - 1 - i) mod 4096 for a fold pivot column p of the case; it is its own inverse and never maps a column to itself.
All inputs are finite; a program needn't handle non-finite values. No bound on the sum of `sea_mask` on one device may be relied on, other than what follows from the above.
Results may differ from a plain program's by a relative error of at most 0.00002.
Values sent between devices are 32-bit elements; how exact they have to be, the bound alone decides.
No kernel may reach another device: no remote copies, remote signals or barrier semaphores. Data moves between devices by JAX's collectives and lax.ppermute only.
A program may use at most 192 MiB of HBM per device.

v0:
```python
import jax
import jax.numpy as jnp
from jax import lax
from jax.sharding import PartitionSpec as P

PASSES = 3


def extended(block, sides, width):
    for axis, dim in sides:
        count = lax.axis_size(axis)
        forward = [(i, i + 1) for i in range(count - 1)]
        forward.append((count - 1, 0))
        backward = [(target, source) for source, target in forward]
        low = lax.ppermute(
            lax.slice_in_dim(block, block.shape[dim] - width, None, axis=dim), axis, forward
        )
        high = lax.ppermute(lax.slice_in_dim(block, 0, width, axis=dim), axis, backward)
        block = jnp.concatenate([low, block, high], axis=dim)
    return block


def diffuse(current, kappa_pad, sea_pad):
    inner_rows = current.shape[-2] - 2
    inner_cols = current.shape[-1] - 2
    centre = current[..., 1:-1, 1:-1]
    kappa_mid = kappa_pad[1:-1, 1:-1]
    sea_mid = sea_pad[..., 1:-1, 1:-1]
    change = jnp.zeros_like(centre)
    for row_off, col_off in ((1, 2), (1, 0), (2, 1), (0, 1)):
        nearby = current[..., row_off : row_off + inner_rows, col_off : col_off + inner_cols]
        kappa_near = kappa_pad[row_off : row_off + inner_rows, col_off : col_off + inner_cols]
        sea_near = sea_pad[..., row_off : row_off + inner_rows, col_off : col_off + inner_cols]
        conduct = 0.5 * (kappa_mid + kappa_near) * sea_mid * sea_near
        change = change + conduct * (nearby - centre)
    return centre + change


def fold_ghost(gathered, rim_width, col_base, col_count, fold_partner):
    flipped = gathered[..., ::-1, :]
    global_count = gathered.shape[-1]
    col_ids = jnp.mod(
        col_base - rim_width + jnp.arange(col_count + 2 * rim_width, dtype=jnp.int32), global_count
    )
    return jnp.take(flipped, jnp.take(fold_partner, col_ids), axis=-1)


def close_rim(padded, ghost_rows, rim_width, top_band, bottom_band, row_count):
    row_ids = jnp.arange(padded.shape[-2])[:, None]
    southern = jnp.logical_and(row_ids < rim_width, bottom_band)
    padded = jnp.where(southern, jnp.zeros_like(padded), padded)
    upper = padded[..., row_count + rim_width :, :]
    return jnp.concatenate(
        [padded[..., : row_count + rim_width, :], jnp.where(top_band, ghost_rows, upper)], axis=-2
    )


def per_device(perturb, control, diffusivity, sea_mask, fold_partner):
    reach_width = PASSES
    row_count = control.shape[2]
    col_count = control.shape[3]
    col_base = lax.axis_index("lon") * col_count
    band_idx = lax.axis_index("lat")
    top_band = band_idx == lax.axis_size("lat") - 1
    bottom_band = band_idx == 0
    sea_float = sea_mask.astype(jnp.float32)
    coeffs = jnp.concatenate([diffusivity[None], sea_float], axis=0)
    coef_pad = extended(coeffs, (("lon", 2), ("lat", 1)), reach_width)
    coef_rows = lax.all_gather(coeffs[:, row_count - reach_width :, :], "lon", axis=2, tiled=True)
    coef_pad = close_rim(
        coef_pad,
        fold_ghost(coef_rows, reach_width, col_base, col_count, fold_partner),
        reach_width,
        top_band,
        bottom_band,
        row_count,
    )
    kappa_pad = coef_pad[0]
    sea_pad = coef_pad[1:]
    fields = control
    kappa_one = kappa_pad[
        reach_width - 1 : reach_width + row_count + 1, reach_width - 1 : reach_width + col_count + 1
    ]
    sea_one = sea_pad[
        :,
        reach_width - 1 : reach_width + row_count + 1,
        reach_width - 1 : reach_width + col_count + 1,
    ]
    for sweep in range(reach_width):
        padded = extended(fields, (("lon", 3), ("lat", 2)), 1)
        folded = lax.all_gather(fields[:, :, row_count - 1 :, :], "lon", axis=3, tiled=True)
        padded = close_rim(
            padded,
            fold_ghost(folded, 1, col_base, col_count, fold_partner),
            1,
            top_band,
            bottom_band,
            row_count,
        )
        fields = diffuse(padded, kappa_one, sea_one)
    partial_value = jnp.sum(perturb * fields, axis=0)
    summed = lax.psum(partial_value, "mem")
    return summed * sea_float


def solution(mesh):
    return jax.shard_map(
        per_device,
        mesh=mesh,
        in_specs=(
            P("mem", None, "lat", "lon"),
            P("mem", None, "lat", "lon"),
            P("lat", "lon"),
            P(None, "lat", "lon"),
            P(),
        ),
        out_specs=P(None, "lat", "lon"),
        check_vma=False,
    )
```

profile of v0, /device:TPU:1, one launch (start us, length us, event | category | flops | bytes accessed | tf_op | source)
XLA Modules:
  0.0 445.4 jit_solution(15654388929011852666)
XLA Ops:
  17.5 4.3 collective-permute-start.5
  21.8 4.9 %fusion.49 = (f32[2,2,1024,1]{3,2,1,0:T(8,128)}, f32[2,2,1024,1]{3,2,1,0:T(8,128)}) fusion(f32[2,2,1024,256]{3,2,1,0:T(8,128)} %param.10), kind=kLoop, calls=%fused_computation.118 | loop fusion | bytes 65536 | tf_op jit(solution)/shard_map/slice | solution.py:16
  31.2 4.8 %collective-permute-start.1 = (f32[2,2,1024,1]{2,1,3,0:T(2,128)S(1)}, f32[2,2,1024,1]{2,1,3,0:T(2,128)S(1)}, u32[]{:S(2)}, u32[]{:S(2)}) collective-permute-start(f32[2,2,1024,1]{2,1,3,0:T(2,128)S(1)} %copy.429), channel_id=1, source_target_pairs={{8,0},{16,8},{24,16},{32,24},{40,32},{48,40},{56,48},{64,56},{72,6... | collective-permute-start | bytes 49160 | tf_op jit(solution)/shard_map/ppermute | solution.py:18
  42.3 15.7 %all_gather.12 = f32[3,3,4096]{2,1,0:T(4,128)S(1)} all-gather(f32[3,3,256]{2,1,0:T(4,128)S(1)} %pad_maximum_fusion.8), channel_id=1, replica_groups=mesh['lon'=16,'lat'=2,'mem'=4] {'lon'}, dimensions={2}, use_global_device_ids=true | all-gather | bytes 156672 | tf_op jit(solution)/shard_map/all_gather | solution.py:69
  58.0 5.4 %copy.372 = f32[2,2,1024,256]{2,3,1,0:T(8,128)} copy(f32[2,2,1024,256]{3,2,1,0:T(8,128)} %param.10) | data formatting | bytes 8388608 | tf_op args[1]
  74.8 18.5 %all_gather.13 = f32[2,2,1,4096]{3,2,1,0:T(1,128)S(1)} all-gather(f32[2,2,1,256]{3,2,1,0:T(1,128)S(1)} %slice.240), channel_id=1, replica_groups=mesh['lon'=16,'lat'=2,'mem'=4] {'lon'}, dimensions={3}, use_global_device_ids=true | all-gather | bytes 69632 | tf_op jit(solution)/shard_map/all_gather | solution.py:91
  93.4 5.9 %copy.383 = f32[3,3,4096]{1,0,2:T(4,128)} copy(f32[3,3,4096]{2,1,0:T(4,128)S(1)} %all_gather.12) | data formatting | bytes 294912 | tf_op jit(solution)/shard_map/all_gather | solution.py:69
  99.3 22.7 %rev.3 = f32[3,3,4096]{1,0,2:T(4,128)} reverse(f32[3,3,4096]{1,0,2:T(4,128)} %copy.383), dimensions={1} | reverse | bytes 294912 | tf_op jit(solution)/shard_map/rev | solution.py:40
  122.0 5.2 %gather_fusion.1 = f32[262,3,3]{2,1,0:T(4,128)} fusion(f32[3,3,4096]{1,0,2:T(4,128)} %rev.3, s32[1024]{0:T(1024)S(1)} %pad_clamp_fusion.2), kind=kCustom, calls=%fused_computation.5 | custom fusion | bytes 19912 | tf_op jit(solution)/shard_map/jit(_take)/gather | solution.py:45
  128.4 4.3 copy.420
  132.8 3.2 gather_fusion.3
  136.0 4.0 copy.390
  142.8 6.7 %concatenate.40 = f32[2,2,1026,258]{2,3,1,0:T(8,128)} concatenate(f32[2,2,1,258]{2,3,1,0:T(8,128)} %copy.376, f32[2,2,1024,258]{2,3,1,0:T(8,128)} %copy-done.5, f32[2,2,1,258]{2,3,1,0:T(8,128)} %copy.377), dimensions={2} | concatenate | bytes 8470656 | tf_op jit(solution)/shard_map/concatenate | solution.py:19
  149.5 4.9 %broadcast_select_fusion = f32[2,2,1026,258]{2,3,1,0:T(8,128)} fusion(f32[2,2,1026,258]{2,3,1,0:T(8,128)} %concatenate.40, pred[1026]{0:T(1024)(128)(4,1)S(1)} %fusion.36), kind=kLoop, calls=%fused_computation.55 | loop fusion | flops 1058832 | bytes 8471682 | tf_op jit(solution)/shard_map/jit(_where)/select_n | solution.py:51
  158.5 3.6 pad_maximum_fusion
  168.9 15.2 %concatenate.43 = f32[3,1030,262]{2,1,0:T(8,128)} concatenate(f32[3,3,262]{2,1,0:T(4,128)S(1)} %collective-permute-done.6, f32[3,1024,262]{2,1,0:T(8,128)} %copy-done.9, f32[3,3,262]{2,1,0:T(4,128)S(1)} %collective-permute-done.7), dimensions={1} | concatenate | bytes 6476640 | tf_op jit(solution)/shard_map/concatenate | solution.py:19
  188.4 5.5 %slice_multiply_fusion.2 = (f32[2,1024,256]{2,1,0:T(8,128)}, f32[2,1024,256]{2,1,0:T(8,128)}, f32[2,1024,256]{2,1,0:T(8,128)}, f32[2,1024,256]{2,1,0:T(8,128)}) fusion(f32[3,1030,262]{2,1,0:T(8,128)S(1)} %broadcast_select_fusion.3, f32[1024,256]{1,0:T(8,128)S(1)} %get-tuple-element.29, f32[1024,256]{1,0:T(8,128)S(1)} %get-tuple-element.32, ...), kind=kLoop, calls=%fused_computation.63 | loop fusion | flops 4718592 | bytes 24209840 | tf_op jit(solution)/shard_map/mul | solution.py:34
  204.5 13.0 %fusion.22 = f32[2,2,1024,256]{2,3,1,0:T(8,128)S(1)} fusion(f32[2,2,1026,258]{2,3,1,0:T(8,128)} %broadcast_select_fusion, f32[2,2,1,258]{2,3,1,0:T(8,128)S(1)} %slice_select_fusion.2, f32[2,2,1025,258]{2,3,1,0:T(8,128)} %bitcast.21, f32[2,1024,256]{1,2,0:T(8,128)} %copy.391, f32[2,1024,256]{1,2,0:T(8,128)} %copy.387, f32[2,1024,256]{1,2,0:T(8,128)} %copy.386, ...), kind=kLoop, calls=%fused_computation.41 | loop fusion | flops 13631488 | bytes 33595456 | tf_op jit(solution)/shard_map/add | solution.py:36
  217.7 4.8 %collective-permute-start.9 = (f32[2,2,1024,1]{2,1,3,0:T(2,128)S(1)}, f32[2,2,1024,1]{2,1,3,0:T(2,128)S(1)}, u32[]{:S(2)}, u32[]{:S(2)}) collective-permute-start(f32[2,2,1024,1]{2,1,3,0:T(2,128)S(1)} %copy.393), channel_id=1, source_target_pairs={{8,0},{16,8},{24,16},{32,24},{40,32},{48,40},{56,48},{64,56},{72,6... | collective-permute-start | bytes 49160 | tf_op jit(solution)/shard_map/ppermute | solution.py:18
  230.7 18.1 %all_gather.14 = f32[2,2,1,4096]{3,1,2,0:T(2,128)S(1)} all-gather(f32[2,2,1,256]{3,1,2,0:T(2,128)S(1)} %copy.401), channel_id=1, replica_groups=mesh['lon'=16,'lat'=2,'mem'=4] {'lon'}, dimensions={3}, use_global_device_ids=true | all-gather | bytes 69632 | tf_op jit(solution)/shard_map/all_gather | solution.py:91
  248.8 4.4 copy.402
  253.2 3.2 gather_fusion.4
  256.4 4.0 copy.404
  260.9 6.6 %concatenate.47 = f32[2,2,1026,258]{2,3,1,0:T(8,128)} concatenate(f32[2,2,1,258]{2,3,1,0:T(8,128)S(1)} %copy.398, f32[2,2,1024,258]{2,3,1,0:T(8,128)} %copy-done.7, f32[2,2,1,258]{2,3,1,0:T(8,128)S(1)} %copy.399), dimensions={2} | concatenate | bytes 8470656 | tf_op jit(solution)/shard_map/concatenate | solution.py:19
  272.0 7.1 %fusion.13 = f32[2,2,1024,256]{2,3,1,0:T(8,128)} fusion(f32[2,2,1026,258]{2,3,1,0:T(8,128)S(1)} %broadcast_select_fusion.1, f32[2,2,1,258]{2,3,1,0:T(8,128)S(1)} %slice_select_fusion.1, f32[2,2,1025,258]{2,3,1,0:T(8,128)S(1)} %bitcast.22, f32[2,1024,256]{1,2,0:T(8,128)S(1)} %copy-done.4, f32[2,1024,256]{1,2,0:T(8,128)S(1)} %copy-done.3, ...), kind=kLoop, calls=%fused_computation.28 | loop fusion | flops 13631488 | bytes 33595456 | tf_op jit(solution)/shard_map/add | solution.py:36
  285.0 5.4 %copy.418 = f32[2,2,1024,256]{2,3,1,0:T(8,128)} copy(f32[2,2,1024,256]{3,2,1,0:T(8,128)} %param.9) | data formatting | bytes 8388608 | tf_op args[0]
  298.9 16.9 %all_gather.15 = f32[2,2,1,4096]{3,1,2,0:T(2,128)S(1)} all-gather(f32[2,2,1,256]{3,1,2,0:T(2,128)S(1)} %copy.414), channel_id=1, replica_groups=mesh['lon'=16,'lat'=2,'mem'=4] {'lon'}, dimensions={3}, use_global_device_ids=true | all-gather | bytes 69632 | tf_op jit(solution)/shard_map/all_gather | solution.py:91
  315.8 4.4 copy.415
  323.4 4.0 copy.417
  327.9 6.6 %concatenate.50 = f32[2,2,1026,258]{2,3,1,0:T(8,128)} concatenate(f32[2,2,1,258]{2,3,1,0:T(8,128)S(1)} %copy.411, f32[2,2,1024,258]{2,3,1,0:T(8,128)} %copy-done.6, f32[2,2,1,258]{2,3,1,0:T(8,128)S(1)} %copy.412), dimensions={2} | concatenate | bytes 8470656 | tf_op jit(solution)/shard_map/concatenate | solution.py:19
  337.5 9.6 %fusion.4 = f32[2,1024,256]{1,2,0:T(8,128)} fusion(f32[2,2,1024,256]{2,3,1,0:T(8,128)} %copy.418, f32[2,2,1026,258]{2,3,1,0:T(8,128)S(1)} %broadcast_select_fusion.2, f32[2,2,1,258]{2,3,1,0:T(8,128)S(1)} %slice_select_fusion, f32[2,2,1025,258]{2,3,1,0:T(8,128)S(1)} %bitcast.23, f32[2,1024,256]{1,2,0:T(8,128)} %copy.391, f32[2,1024,256]{1,2,0:T(8,128)} %copy.387, ...), kind=kLoop, calls=%fused_computation.15 | loop fusion | flops 15204352 | bytes 35692608 | tf_op jit(solution)/shard_map/reduce_sum | solution.py:101
  350.2 85.0 %all-reduce.2.cloned.1.call-done = f32[2,1024,256]{2,1,0:T(8,128)} async-done(((f32[2,1024,256]{2,1,0:T(8,128)}), f32[2,1024,256]{2,1,0:T(8,128)}) %all-reduce.2.cloned.1.call-update) | async-done | bytes 2097168 | tf_op jit(solution)/shard_map/psum | solution.py:102
  (142 shorter events, 103.6 us)
Async XLA Ops:
  6.5 29.5 %copy-start = (s32[4096]{0:T(1024)S(1)}, s32[4096]{0:T(1024)}, u32[]{:S(2)}) copy-start(s32[4096]{0:T(1024)} %param.13) | copy-start | bytes 49156
  6.5 428.6 %all-reduce.2.cloned.1.call-start = ((), (), s32[]{:S(2)}) async-start(), calls=%async_computation | async-start | bytes 4194304 | tf_op jit(solution)/shard_map/psum | solution.py:102
  12.5 141.9 %collective-permute-start.4 = (f32[3,1024,3]{1,2,0:T(4,128)S(1)}, f32[3,1024,3]{1,2,0:T(4,128)S(1)}, u32[]{:S(2)}, u32[]{:S(2)}) collective-permute-start(f32[3,1024,3]{1,2,0:T(4,128)S(1)} %copy.379), channel_id=1, source_target_pairs={{0,8},{8,16},{16,24},{24,32},{32,40},{40,48},{48,56},{56,64},{64,7... | collective-permute-start | bytes 110600 | tf_op jit(solution)/shard_map/ppermute | solution.py:15
  17.5 138.6 %collective-permute-start.5 = (f32[3,1024,3]{1,2,0:T(4,128)}, f32[3,1024,3]{1,2,0:T(4,128)}, u32[]{:S(2)}, u32[]{:S(2)}) collective-permute-start(f32[3,1024,3]{1,2,0:T(4,128)} %copy.380), channel_id=1, source_target_pairs={{8,0},{16,8},{24,16},{32,24},{40,32},{48,40},{56,48},{64,56},{72,6... | collective-permute-start | bytes 110600 | tf_op jit(solution)/shard_map/ppermute | solution.py:18
  28.9 35.2 %collective-permute-start = (f32[2,2,1024,1]{2,1,3,0:T(2,128)S(1)}, f32[2,2,1024,1]{2,1,3,0:T(2,128)S(1)}, u32[]{:S(2)}, u32[]{:S(2)}) collective-permute-start(f32[2,2,1024,1]{2,1,3,0:T(2,128)S(1)} %copy.428), channel_id=1, source_target_pairs={{0,8},{8,16},{16,24},{24,32},{32,40},{40,48},{48,56},{56,64},{64,7... | collective-permute-start | bytes 49160 | tf_op jit(solution)/shard_map/ppermute | solution.py:15
  31.2 33.0 %collective-permute-start.1 = (f32[2,2,1024,1]{2,1,3,0:T(2,128)S(1)}, f32[2,2,1024,1]{2,1,3,0:T(2,128)S(1)}, u32[]{:S(2)}, u32[]{:S(2)}) collective-permute-start(f32[2,2,1024,1]{2,1,3,0:T(2,128)S(1)} %copy.429), channel_id=1, source_target_pairs={{8,0},{16,8},{24,16},{32,24},{40,32},{48,40},{56,48},{64,56},{72,6... | collective-permute-start | bytes 49160 | tf_op jit(solution)/shard_map/ppermute | solution.py:18
  71.4 68.6 %collective-permute-start.2 = (f32[2,2,1,258]{3,1,2,0:T(2,128)S(1)}, f32[2,2,1,258]{3,1,2,0:T(2,128)S(1)}, u32[]{:S(2)}, u32[]{:S(2)}) collective-permute-start(f32[2,2,1,258]{3,1,2,0:T(2,128)S(1)} %copy.374), channel_id=1, source_target_pairs={{0,4},{4,0},{1,5},{5,1},{2,6},{6,2},{3,7},{7,3},{8,12},{12,8},{9,1... | collective-permute-start | bytes 12392 | tf_op jit(solution)/shard_map/ppermute | solution.py:15
  74.7 66.4 %collective-permute-start.3 = (f32[2,2,1,258]{3,1,2,0:T(2,128)}, f32[2,2,1,258]{3,1,2,0:T(2,128)}, u32[]{:S(2)}, u32[]{:S(2)}) collective-permute-start(f32[2,2,1,258]{3,1,2,0:T(2,128)} %copy.375), channel_id=1, source_target_pairs={{4,0},{0,4},{5,1},{1,5},{6,2},{2,6},{7,3},{3,7},{12,8},{8,12},{13,... | collective-permute-start | bytes 12392 | tf_op jit(solution)/shard_map/ppermute | solution.py:18
  158.5 7.9 %copy-start.12 = (f32[2,2,1,258]{2,3,1,0:T(8,128)S(1)}, f32[2,2,1,258]{2,3,1,0:T(8,128)}, u32[]{:S(2)}) copy-start(f32[2,2,1,258]{2,3,1,0:T(8,128)} %copy.390) | copy-start | bytes 12388
  158.5 7.9 %copy-start.15 = (pred[258]{0:T(512)(128)(4,1)S(1)}, pred[258]{0:T(512)(128)(4,1)}, u32[]{:S(2)}) copy-start(pred[258]{0:T(512)(128)(4,1)} %get-tuple-element.6) | copy-start | bytes 778
  162.2 2.2 copy-start.9
  164.4 3.4 collective-permute-start.6
  165.8 3.1 collective-permute-start.7
  167.8 16.3 %copy-start.16 = (pred[1030]{0:T(1024)(128)(4,1)S(1)}, pred[1030]{0:T(1024)(128)(4,1)}, u32[]{:S(2)}) copy-start(pred[1030]{0:T(1024)(128)(4,1)} %fusion.37) | copy-start | bytes 3094
  184.1 2.7 copy-start.17
  217.5 5.0 %copy-start.8 = (f32[2,2,1024,256]{2,3,1,0:T(8,128)}, f32[2,2,1024,256]{2,3,1,0:T(8,128)S(1)}, u32[]{:S(2)}) copy-start(f32[2,2,1024,256]{2,3,1,0:T(8,128)S(1)} %fusion.22) | copy-start | bytes 12582916
  217.6 6.0 %collective-permute-start.8 = (f32[2,2,1024,1]{2,1,3,0:T(2,128)S(1)}, f32[2,2,1024,1]{2,1,3,0:T(2,128)S(1)}, u32[]{:S(2)}, u32[]{:S(2)}) collective-permute-start(f32[2,2,1024,1]{2,1,3,0:T(2,128)S(1)} %copy.392), channel_id=1, source_target_pairs={{0,8},{8,16},{16,24},{24,32},{32,40},{40,48},{48,56},{56,64},{64,7... | collective-permute-start | bytes 49160 | tf_op jit(solution)/shard_map/ppermute | solution.py:15
  217.7 5.9 %collective-permute-start.9 = (f32[2,2,1024,1]{2,1,3,0:T(2,128)S(1)}, f32[2,2,1024,1]{2,1,3,0:T(2,128)S(1)}, u32[]{:S(2)}, u32[]{:S(2)}) collective-permute-start(f32[2,2,1024,1]{2,1,3,0:T(2,128)S(1)} %copy.393), channel_id=1, source_target_pairs={{8,0},{16,8},{24,16},{32,24},{40,32},{48,40},{56,48},{64,56},{72,6... | collective-permute-start | bytes 49160 | tf_op jit(solution)/shard_map/ppermute | solution.py:18
  226.4 2.1 copy-start.7
  228.9 31.5 %collective-permute-start.10 = (f32[2,2,1,258]{3,1,2,0:T(2,128)S(1)}, f32[2,2,1,258]{3,1,2,0:T(2,128)S(1)}, u32[]{:S(2)}, u32[]{:S(2)}) collective-permute-start(f32[2,2,1,258]{3,1,2,0:T(2,128)S(1)} %copy.396), channel_id=1, source_target_pairs={{0,4},{4,0},{1,5},{5,1},{2,6},{6,2},{3,7},{7,3},{8,12},{12,8},{9,1... | collective-permute-start | bytes 12392 | tf_op jit(solution)/shard_map/ppermute | solution.py:15
  229.4 31.2 %collective-permute-start.11 = (f32[2,2,1,258]{3,1,2,0:T(2,128)S(1)}, f32[2,2,1,258]{3,1,2,0:T(2,128)S(1)}, u32[]{:S(2)}, u32[]{:S(2)}) collective-permute-start(f32[2,2,1,258]{3,1,2,0:T(2,128)S(1)} %copy.397), channel_id=1, source_target_pairs={{4,0},{0,4},{5,1},{1,5},{6,2},{2,6},{7,3},{3,7},{12,8},{8,12},{13,... | collective-permute-start | bytes 12392 | tf_op jit(solution)/shard_map/ppermute | solution.py:18
  267.5 2.9 copy-start.14
  267.5 3.2 copy-start.2
  267.5 3.9 copy-start.3
  267.5 4.5 %copy-start.4 = (f32[2,1024,256]{1,2,0:T(8,128)S(1)}, f32[2,1024,256]{1,2,0:T(8,128)}, u32[]{:S(2)}) copy-start(f32[2,1024,256]{1,2,0:T(8,128)} %copy.391) | copy-start | bytes 6291460
  280.0 11.7 %collective-permute-start.12 = (f32[2,2,1024,1]{2,1,3,0:T(2,128)S(1)}, f32[2,2,1024,1]{2,1,3,0:T(2,128)S(1)}, u32[]{:S(2)}, u32[]{:S(2)}) collective-permute-start(f32[2,2,1024,1]{2,1,3,0:T(2,128)S(1)} %copy.405), channel_id=1, source_target_pairs={{0,8},{8,16},{16,24},{24,32},{32,40},{40,48},{48,56},{56,64},{64,7... | collective-permute-start | bytes 49160 | tf_op jit(solution)/shard_map/ppermute | solution.py:15
  281.9 9.9 %collective-permute-start.13 = (f32[2,2,1024,1]{2,1,3,0:T(2,128)S(1)}, f32[2,2,1024,1]{2,1,3,0:T(2,128)S(1)}, u32[]{:S(2)}, u32[]{:S(2)}) collective-permute-start(f32[2,2,1024,1]{2,1,3,0:T(2,128)S(1)} %copy.406), channel_id=1, source_target_pairs={{8,0},{16,8},{24,16},{32,24},{40,32},{48,40},{56,48},{64,56},{72,6... | collective-permute-start | bytes 49160 | tf_op jit(solution)/shard_map/ppermute | solution.py:18
  297.1 30.3 %collective-permute-start.14 = (f32[2,2,1,258]{3,1,2,0:T(2,128)S(1)}, f32[2,2,1,258]{3,1,2,0:T(2,128)S(1)}, u32[]{:S(2)}, u32[]{:S(2)}) collective-permute-start(f32[2,2,1,258]{3,1,2,0:T(2,128)S(1)} %copy.409), channel_id=1, source_target_pairs={{0,4},{4,0},{1,5},{5,1},{2,6},{6,2},{3,7},{7,3},{8,12},{12,8},{9,1... | collective-permute-start | bytes 12392 | tf_op jit(solution)/shard_map/ppermute | solution.py:15
  297.6 30.1 %collective-permute-start.15 = (f32[2,2,1,258]{3,1,2,0:T(2,128)S(1)}, f32[2,2,1,258]{3,1,2,0:T(2,128)S(1)}, u32[]{:S(2)}, u32[]{:S(2)}) collective-permute-start(f32[2,2,1,258]{3,1,2,0:T(2,128)S(1)} %copy.410), channel_id=1, source_target_pairs={{4,0},{0,4},{5,1},{1,5},{6,2},{2,6},{7,3},{3,7},{12,8},{8,12},{13,... | collective-permute-start | bytes 12392 | tf_op jit(solution)/shard_map/ppermute | solution.py:18
  334.5 2.8 copy-start.13
  347.1 88.0 %copy-start.11 = (s32[2,1024,256]{2,1,0:T(8,128)S(1)}, s32[2,1024,256]{2,1,0:T(8,128)}, u32[]{:S(2)}) copy-start(s32[2,1024,256]{2,1,0:T(8,128)} %param.12) | copy-start | bytes 6291460
  350.1 88.2 %copy-start.1 = (s32[4096]{0:T(1024)S(1)}, s32[4096]{0:T(1024)}, u32[]{:S(2)}) copy-start(s32[4096]{0:T(1024)} %param.13) | copy-start | bytes 49156
  (3 other events, 6.0 us)
Sparse Core Ops, SparseCore 0:
  350.3 84.7 all-reduce.1
where the time goes:
time: 454 us; the launch traced here: 445 us
  local copies, waits for them, and re-layouts  175 us (39%)
  waiting for transfers between devices  86.8 us (19%)
  other arithmetic  72.6 us (16%)
  blocking collectives  69.2 us (15%)
  starting transfers between devices  28.2 us (6%)
  between operations  14.1 us (3%)
    psum x1, waiting for transfers between devices, per_device(): summed = lax.psum(partial_value, 'mem')  85 us
    all_gather x3, blocking collectives, per_device(): lax.all_gather(fields[:, :, row_count - 1:, :], 'lon', axis=3, tiled=True)  53.5 us
    concatenate x4, local copies, waits for them, and re-layouts, extended(): block = jnp.concatenate([low, block, high], axis=dim)  35 us
    gather x10, local copies, waits for them, and re-layouts, fold_ghost(): return jnp.take(flipped, jnp.take(fold_partner, col_ids), axis=-1)  32.5 us
    unnamed x41, local copies, waits for them, and re-layouts  28 us
    rev x1, local copies, waits for them, and re-layouts, fold_ghost(): flipped = gathered[..., ::-1, :]  22.7 us
    ppermute x8, starting transfers between devices, extended(): lax.ppermute(lax.slice_in_dim(block, 0, width, axis=dim), axis, backward)  20.5 us
    add x2, other arithmetic, diffuse(): return centre + change  20.1 us
  transfers between devices with their start and end apart: 17, of which 3 were waited for; matrix products, arithmetic and copies ran while one was open for 28% of the time, Pallas kernels for 0%

commit v1 on v0

v1 whole, which is shorter than its diff:
```python
import functools

import jax
import jax.numpy as jnp
from jax import lax
from jax.experimental import pallas as pl
from jax.experimental.pallas import tpu as pltpu
from jax.sharding import PartitionSpec as P

PASSES = 3
LANES = 128
TILE = 8
FIELDS = 7
PITCH = 16
GROUPS = 5
STEP = 16
F32 = jnp.float32
MIB = 1 << 20


def lane_ids(rows):
    return lax.broadcasted_iota(jnp.int32, (rows, LANES), 1)


def spin(value, shift):
    shift %= LANES
    return value if shift == 0 else pltpu.roll(value, shift, 1)


def east_of(tiles):
    turned = [spin(v, -1) for v in tiles]
    last = lane_ids(tiles[0].shape[0]) == LANES - 1
    return [
        jnp.where(last, turned[t + 1], turned[t]) if t + 1 < len(tiles) else turned[t]
        for t in range(len(tiles))
    ]


def west_of(tiles):
    turned = [spin(v, 1) for v in tiles]
    first = lane_ids(tiles[0].shape[0]) == 0
    return [jnp.where(first, turned[t - 1], turned[t]) if t else turned[t] for t in range(len(tiles))]


def conductances(kappa, sea, diag, g_east, g_west, g_north, low, high):
    tiles = range(kappa.shape[0])
    for r in range(low, high, STEP):
        k = [kappa[t, r : r + STEP, :] for t in tiles]
        s = [sea[t, r : r + STEP, :].astype(F32) for t in tiles]
        k_east, s_east = east_of(k), east_of(s)
        east = [0.5 * (k[t] + k_east[t]) * s[t] * s_east[t] for t in tiles]
        west = west_of(east)
        for t in tiles:
            k_n, s_n = kappa[t, r + 1 : r + STEP + 1, :], sea[t, r + 1 : r + STEP + 1, :].astype(F32)
            k_s, s_s = kappa[t, r - 1 : r + STEP - 1, :], sea[t, r - 1 : r + STEP - 1, :].astype(F32)
            north = 0.5 * (k[t] + k_n) * s[t] * s_n
            south = 0.5 * (k[t] + k_s) * s[t] * s_s
            diag[t, r : r + STEP, :] = 1.0 - ((east[t] + west[t]) + (north + south))
            g_east[t, r : r + STEP, :] = east[t]
            g_west[t, r : r + STEP, :] = west[t]
            g_north[t, r : r + STEP, :] = north


def diffused(field, coefs, r, member):
    diag, g_east, g_west, g_north = coefs
    tiles = range(diag.shape[0])
    here = [field[member, t, r : r + STEP, :] for t in tiles]
    east, west = east_of(here), west_of(here)
    out = []
    for t in tiles:
        north = field[member, t, r + 1 : r + STEP + 1, :]
        south = field[member, t, r - 1 : r + STEP - 1, :]
        out.append(
            (diag[t, r : r + STEP, :] * here[t])
            + (g_east[t, r : r + STEP, :] * east[t] + g_west[t, r : r + STEP, :] * west[t])
            + (g_north[t, r : r + STEP, :] * north + g_north[t, r - 1 : r + STEP - 1, :] * south)
        )
    return out


def sweep(source, target, coefs, low, high):
    for r in range(low, high, STEP):
        for member in range(source.shape[0]):
            for t, value in enumerate(diffused(source, coefs, r, member)):
                target[member, t, r : r + STEP, :] = value


def started(copies):
    for copy in copies:
        copy.start()
    return copies


def finish(copies):
    for copy in copies:
        copy.wait()


def band_kernel(keep, low, rows, has_rim, core, control, perturb, kappa, mask, *rest):
    rest = list(rest)
    rim = rest.pop(0) if has_rim else None
    other = rest.pop(0) if keep else None
    out, c_buf, v_buf, p_buf, k_buf, s_buf, diag, g_east, g_west, g_north, sems = rest
    level = core[0] if keep else 1 - core[0]
    total = control.shape[2]
    first, last = max(low - TILE, 0), min(low + rows + TILE, total)
    at = first - low + 2 * TILE
    count = last - first
    sem = iter(range(sems.shape[0]))
    early, late = [], []
    for t in range(2):
        cols = pl.ds(t * LANES, LANES)
        span, put = pl.ds(first, count), pl.ds(at, count)
        early.append(pltpu.make_async_copy(kappa.at[span, cols], k_buf.at[t, put], sems.at[next(sem)]))
        early.append(pltpu.make_async_copy(mask.at[level, span, cols], s_buf.at[t, put], sems.at[next(sem)]))
    for m in range(2):
        for t in range(2):
            cols = pl.ds(t * LANES, LANES)
            late.append(
                pltpu.make_async_copy(
                    control.at[m, level, pl.ds(first, count), cols],
                    c_buf.at[m, t, pl.ds(at, count)],
                    sems.at[next(sem)],
                )
            )
    for m in range(2):
        for t in range(2):
            cols = pl.ds(t * LANES, LANES)
            late.append(
                pltpu.make_async_copy(
                    perturb.at[m, level, pl.ds(low, rows), cols], p_buf.at[m, t], sems.at[next(sem)]
                )
            )
    started(early)
    started(late)
    finish(early)
    top = rows + 3 * TILE
    coefs = (diag, g_east, g_west, g_north)
    conductances(k_buf, s_buf, *coefs, TILE, top)
    finish(late)
    sweep(c_buf, v_buf, coefs, TILE, top)
    sweep(v_buf, c_buf, coefs, TILE, top)
    for r in range(2 * TILE, rows + 2 * TILE, STEP):
        one, two = (diffused(c_buf, coefs, r, m) for m in range(2))
        for t in range(2):
            q = r - 2 * TILE
            value = one[t] * p_buf[0, t, q : q + STEP, :] + two[t] * p_buf[1, t, q : q + STEP, :]
            value = value * s_buf[t, r : r + STEP, :].astype(F32)
            w = t * rows + q
            if keep:
                value = value + other[w : w + STEP, :]
            out[w : w + STEP, :] = value
    if has_rim:
        value = rim[...]
        if keep:
            value = value + other[2 * rows :, :]
        out[2 * rows :, :] = value


def band(keep, low, rows, core, control, perturb, kappa, mask, rim=None, other=None):
    extra = 0 if rim is None else rim.shape[0]
    operands = [core, control, perturb, kappa, mask]
    specs = [pl.BlockSpec(memory_space=pltpu.SMEM)] + [pl.BlockSpec(memory_space=pl.ANY)] * 4
    for value in (rim, other):
        if value is not None:
            operands.append(value)
            specs.append(pl.BlockSpec(memory_space=pltpu.VMEM))
    high = rows + 4 * TILE
    return pl.pallas_call(
        functools.partial(band_kernel, keep, low, rows, rim is not None),
        out_shape=jax.ShapeDtypeStruct((2 * rows + extra, LANES), F32),
        in_specs=specs,
        out_specs=pl.BlockSpec(memory_space=pltpu.VMEM),
        scratch_shapes=[
            pltpu.VMEM((2, 2, high, LANES), F32),
            pltpu.VMEM((2, 2, high, LANES), F32),
            pltpu.VMEM((2, 2, rows, LANES), F32),
            pltpu.VMEM((2, high, LANES), F32),
            pltpu.VMEM((2, high, LANES), jnp.int32),
        ]
        + [pltpu.VMEM((2, high, LANES), F32)] * 4
        + [pltpu.SemaphoreType.DMA((12,))],
        compiler_params=pltpu.CompilerParams(vmem_limit_bytes=24 * MIB),
        cost_estimate=pl.CostEstimate(flops=rows * 256 * 200, bytes_accessed=rows * 256 * 32, transcendentals=0),
        name="band_keep" if keep else "band_send",
    )(*operands)


def edge_kernel(place, c_low, c_high, k_low, k_high, s_low, s_high, low, high, message):
    for c, k, s, out in ((c_low, k_low, s_low, low), (c_high, k_high, s_high, high)):
        for m in range(2):
            for v in range(2):
                out[2 * m + v] = c[m, v]
        out[4] = k[...]
        out[5] = s[0].astype(F32)
        out[6] = s[1].astype(F32)
    message[...] = jnp.where(place[0] == 0, high[...], low[...])


def edges(place, control, kappa, mask):
    rows, cols = kappa.shape
    end = rows // TILE - 1
    shape = jax.ShapeDtypeStruct((FIELDS, TILE, cols), F32)
    specs = [pl.BlockSpec(memory_space=pltpu.SMEM)]
    specs += [pl.BlockSpec((2, 2, TILE, cols), lambda i, b=b: (0, 0, b, 0)) for b in (0, end)]
    specs += [pl.BlockSpec((TILE, cols), lambda i, b=b: (b, 0)) for b in (0, end)]
    specs += [pl.BlockSpec((2, TILE, cols), lambda i, b=b: (0, b, 0)) for b in (0, end)]
    return pl.pallas_call(
        edge_kernel,
        grid=(1,),
        out_shape=[shape] * 3,
        in_specs=specs,
        out_specs=[pl.BlockSpec((FIELDS, TILE, cols), lambda i: (0, 0, 0))] * 3,
        compiler_params=pltpu.CompilerParams(vmem_limit_bytes=8 * MIB),
        name="edge_rows",
    )(place, control, control, kappa, kappa, mask, mask)


def strips(left, right):
    rows = left[0].shape[0]
    lane = lane_ids(rows)
    west, east = jnp.zeros((rows, LANES), F32), jnp.zeros((rows, LANES), F32)
    for f in range(FIELDS):
        base = PITCH * f
        inside = jnp.logical_and(lane >= base + 3, lane < base + 9)
        west = jnp.where(inside, spin(left[f], base + 3), west)
        inside = jnp.logical_and(lane >= base, lane < base + 6)
        east = jnp.where(inside, spin(right[f], base - (LANES - 6)), east)
    return west, east


def strip_kernel(place, control, kappa, mask, low_rows, fold_a, fold_b, west, east, to_east, to_west, south, north,
                 c_buf, k_buf, s_buf, sems):
    rows = kappa.shape[0]
    parts = 4
    size = rows // parts
    copies = []
    for i in range(parts):
        span = pl.ds(i * size, size)
        copies.append(
            [
                pltpu.make_async_copy(control.at[:, :, span], c_buf.at[:, :, span], sems.at[3 * i]),
                pltpu.make_async_copy(kappa.at[span], k_buf.at[span], sems.at[3 * i + 1]),
                pltpu.make_async_copy(mask.at[:, span], s_buf.at[:, span], sems.at[3 * i + 2]),
            ]
        )
    for part in copies:
        started(part)
    bottom = place[0] == 0
    shift = place[1]
    lane = lane_ids(TILE)
    for f in range(FIELDS):
        south[f] = jnp.where(bottom, 0.0, low_rows[f])
        blocks = []
        for source in (fold_b, fold_a):
            for t in range(2):
                tile = source[f, :, t * LANES : (t + 1) * LANES]
                blocks.append(jnp.concatenate([tile[TILE - 1 - r : TILE - r] for r in range(TILE)], axis=0))
        for t in range(2):
            wanted = 2 * LANES + shift - t * LANES - lane
            inner, outer = wanted % LANES, wanted // LANES
            ghost = jnp.zeros((TILE, LANES), F32)
            for n, block in enumerate(blocks):
                turned = jnp.take_along_axis(block, inner, axis=1, mode="promise_in_bounds")
                ghost = jnp.where(outer == n, turned, ghost)
            part = slice(t * LANES, (t + 1) * LANES)
            north[f, :, part] = jnp.where(bottom, low_rows[f, :, part], ghost)
    for at, source in ((0, south), (rows + TILE, north)):
        left, right = strips(
            [source[f, :, :LANES] for f in range(FIELDS)], [source[f, :, LANES:] for f in range(FIELDS)]
        )
        west[at : at + TILE, :] = left
        east[at : at + TILE, :] = right
    for i in range(parts):
        finish(copies[i])
        for r in range(i * size, (i + 1) * size, STEP):
            halves = []
            for t in range(2):
                part = slice(t * LANES, (t + 1) * LANES)
                values = [c_buf[m, v, r : r + STEP, part] for m in range(2) for v in range(2)]
                values.append(k_buf[r : r + STEP, part])
                values += [s_buf[v, r : r + STEP, part].astype(F32) for v in range(2)]
                halves.append(values)
            left, right = strips(*halves)
            west[r + TILE : r + TILE + STEP, :] = left
            east[r + TILE : r + TILE + STEP, :] = right
    tiles = (rows + 2 * TILE) // TILE // GROUPS
    phase = lane % PITCH
    for source, target in ((east, to_east), (west, to_west)):
        for k in range(tiles):
            value = jnp.zeros((TILE, LANES), F32)
            for g in range(GROUPS):
                r = (g * tiles + k) * TILE
                inside = jnp.logical_and(phase >= 3 * g, phase < 3 * g + 3)
                value = jnp.where(inside, spin(source[r : r + TILE, :], 3 * g - 3), value)
            target[k * TILE : (k + 1) * TILE, :] = value


def pack_strips(place, control, kappa, mask, low_rows, fold_a, fold_b):
    rows, cols = kappa.shape
    tall = rows + 2 * TILE
    vmem = pl.BlockSpec(memory_space=pltpu.VMEM)
    anywhere = pl.BlockSpec(memory_space=pl.ANY)
    return pl.pallas_call(
        strip_kernel,
        out_shape=[jax.ShapeDtypeStruct((tall, LANES), F32)] * 2
        + [jax.ShapeDtypeStruct((tall // GROUPS, LANES), F32)] * 2
        + [jax.ShapeDtypeStruct((FIELDS, TILE, cols), F32)] * 2,
        in_specs=[pl.BlockSpec(memory_space=pltpu.SMEM)] + [anywhere] * 3 + [vmem] * 3,
        out_specs=[vmem] * 6,
        scratch_shapes=[
            pltpu.VMEM((2, 2, rows, cols), F32),
            pltpu.VMEM((rows, cols), F32),
            pltpu.VMEM((2, rows, cols), jnp.int32),
            pltpu.SemaphoreType.DMA((12,)),
        ],
        compiler_params=pltpu.CompilerParams(vmem_limit_bytes=24 * MIB),
        name="pack_strips",
    )(place, control, kappa, mask, low_rows, fold_a, fold_b)


def rim_kernel(core, west_in, east_in, from_west, from_east, low, high, south, north, perturb, keep, send,
               field, spare, kappa, mask, diag, g_east, g_west, g_north, r_field, r_spare, r_kappa, r_mask,
               r_diag, r_east, r_west, r_north, p_buf, sems):
    rows = perturb.shape[2]
    tall = rows + 2 * TILE
    copies = [
        pltpu.make_async_copy(perturb.at[m, v], p_buf.at[m, v], sems.at[2 * m + v]) for m in range(2) for v in range(2)
    ]
    started(copies)
    made = []
    for side, (under, over) in enumerate(((south, low), (high, north))):
        for t in range(2):
            part = slice(t * LANES, (t + 1) * LANES)
            for half, source in enumerate((under, over)):
                at = slice(TILE * (1 + half), TILE * (2 + half))
                for f in range(4):
                    r_field[2 * side + f % 2, f // 2, t, at, :] = source[f, :, part]
                r_kappa[side, t, at, :] = source[4, :, part]
                for v in range(2):
                    r_mask[2 * side + v, t, at, :] = source[5 + v, :, part]
        for v in range(2):
            n = 2 * side + v
            coefs = tuple(ref.at[n] for ref in (r_diag, r_east, r_west, r_north))
            conductances(r_kappa.at[side], r_mask.at[n], *coefs, TILE, 3 * TILE)
            sweep(r_field.at[n], r_spare.at[n], coefs, TILE, 3 * TILE)
            sweep(r_spare.at[n], r_field.at[n], coefs, TILE, 3 * TILE)
            sweep(r_field.at[n], r_spare.at[n], coefs, TILE, 3 * TILE)
    tiles = tall // TILE // GROUPS
    lane = lane_ids(TILE)
    phase = lane % PITCH
    strip = lane // PITCH
    for side, (own, message, at) in enumerate(((west_in, from_west, 0), (east_in, from_east, 6))):
        inside = jnp.logical_and(phase >= at, phase < at + 3)
        for i in range(tall // TILE):
            g, k = i // tiles, i % tiles
            value = jnp.where(
                inside, spin(message[k * TILE : (k + 1) * TILE, :], at - 3 * g), own[i * TILE : (i + 1) * TILE, :]
            )
            put = slice((i + 1) * TILE, (i + 2) * TILE)
            field[side, 0, 0, put, :] = value
            spread = spin(value, -4 * PITCH)
            for f in range(1, 4):
                spread = jnp.where(strip == f, spin(value, (f - 4) * PITCH), spread)
            kappa[side, 0, put, :] = spread
            mask[side, 0, put, :] = jnp.where(strip < 2, spin(value, -5 * PITCH), spin(value, -3 * PITCH))
        coefs = tuple(ref.at[side] for ref in (diag, g_east, g_west, g_north))
        conductances(kappa.at[side], mask.at[side], *coefs, TILE, tall + TILE)
        sweep(field.at[side], spare.at[side], coefs, TILE, tall + TILE)
        sweep(spare.at[side], field.at[side], coefs, TILE, tall + TILE)
    finish(copies)
    mine = core[0] == 0

    def give(at, value):
        put = slice(at, at + TILE)
        keep[put, :] = jnp.where(mine, value[0], value[1])
        send[put, :] = jnp.where(mine, value[1], value[0])

    def product(side, r):
        coefs = tuple(ref.at[side] for ref in (diag, g_east, g_west, g_north))
        value = diffused(field.at[side], coefs, r + 2 * TILE, 0)[0]
        value = value * mask[side, 0, r + 2 * TILE : r + 2 * TILE + STEP, :]
        weight = jnp.zeros((STEP, LANES), F32)
        wide = lane_ids(STEP)
        part = slice(LANES, 2 * LANES) if side else slice(0, LANES)
        for f in range(4):
            base = PITCH * f
            source = p_buf[f // 2, f % 2, r : r + STEP, part]
            weight = jnp.where(
                jnp.logical_and(wide >= base + 3, wide < base + 6),
                spin(source, base + 3 - (LANES - 3 if side else 0)),
                weight,
            )
        value = value * weight
        return value + spin(value, -2 * PITCH)

    groups = LANES // TILE
    block = rows // groups
    for r in range(0, block, STEP):
        values = [jnp.zeros((STEP, LANES), F32) for _ in range(2)]
        wide = lane_ids(STEP)
        for g in range(groups):
            for side in range(2):
                value = product(side, g * block + r)
                at = TILE * g + 5 * side
                inside = jnp.logical_and(wide >= at, wide < at + 3)
                for v in range(2):
                    values[v] = jnp.where(inside, spin(value, at - 3 - PITCH * v), values[v])
        for half in range(0, STEP, TILE):
            give(r + half, [value[half : half + TILE] for value in values])
    south_part = lax.broadcasted_iota(jnp.int32, (TILE, LANES), 0) < TILE // 2
    for t in range(2):
        part = slice(t * LANES, (t + 1) * LANES)
        values = []
        for v in range(2):
            ends = []
            for side, (r, at) in enumerate(((0, TILE * 2), (rows - TILE, TILE))):
                n = 2 * side + v
                total = sum(r_spare[n, m, t, at : at + TILE, :] * p_buf[m, v, r : r + TILE, part] for m in range(2))
                ends.append(total * r_mask[n, t, at : at + TILE, :])
            values.append(jnp.where(south_part, ends[0], ends[1]))
        give(block + TILE * t, values)


def rim_sums(core, west, east, from_west, from_east, low, high, south, north, perturb):
    rows, cols = perturb.shape[2:]
    tall = rows + 4 * TILE
    size = rows * TILE // LANES + 2 * TILE
    vmem = pl.BlockSpec(memory_space=pltpu.VMEM)
    strip = pltpu.VMEM((2, 1, tall, LANES), F32)
    row = pltpu.VMEM((4, 2, 4 * TILE, LANES), F32)
    return pl.pallas_call(
        rim_kernel,
        out_shape=[jax.ShapeDtypeStruct((size, LANES), F32)] * 2,
        in_specs=[pl.BlockSpec(memory_space=pltpu.SMEM)] + [vmem] * 8 + [pl.BlockSpec(memory_space=pl.ANY)],
        out_specs=[vmem] * 2,
        scratch_shapes=[pltpu.VMEM((2, 1, 1, tall, LANES), F32)] * 2
        + [strip] * 6
        + [pltpu.VMEM((4, 2, 2, 4 * TILE, LANES), F32)] * 2
        + [pltpu.VMEM((2, 2, 4 * TILE, LANES), F32)]
        + [row] * 5
        + [pltpu.VMEM((2, 2, rows, cols), F32), pltpu.SemaphoreType.DMA((4,))],
        compiler_params=pltpu.CompilerParams(vmem_limit_bytes=24 * MIB),
        name="rim_sums",
    )(core, west, east, from_west, from_east, low, high, south, north, perturb)


def close_kernel(bands, core, *rest):
    count = len(bands)
    parts = [rest[4 * j : 4 * j + 4] for j in range(count)]
    out, buf, sems = rest[4 * count :]
    rim_at = 2 * bands[-1][1]
    rows = buf.shape[1]
    block = rows * TILE // LANES
    lane = lane_ids(TILE)
    row = lax.broadcasted_iota(jnp.int32, (TILE, LANES), 0)
    copies = []
    for who in range(2):
        level = core[0] if who == 0 else 1 - core[0]
        last = parts[-1]
        for j, (low, size) in enumerate(bands):
            one, two = parts[j][2 * who], parts[j][2 * who + 1]
            for q in range(0, size, TILE):
                r = low + q
                g, k = r // block, r % block
                side = last[2 * who][rim_at + k : rim_at + k + TILE, :] + last[2 * who + 1][rim_at + k : rim_at + k + TILE, :]
                for t in range(2):
                    at = t * size + q
                    value = one[at : at + TILE, :] + two[at : at + TILE, :]
                    if r in (0, rows - TILE):
                        ra = rim_at + block + TILE * t
                        ends = last[2 * who][ra : ra + TILE, :] + last[2 * who + 1][ra : ra + TILE, :]
                        value = jnp.where(row < 3 if r == 0 else row >= TILE - 3, ends, value)
                    if t == 0:
                        value = jnp.where(lane < 3, spin(side, -TILE * g), value)
                    else:
                        value = jnp.where(lane >= LANES - 3, spin(side, LANES - 8 - TILE * g), value)
                    buf[who, r : r + TILE, t * LANES : (t + 1) * LANES] = value
            span = pl.ds(low, size)
            copy = pltpu.make_async_copy(buf.at[who, span], out.at[level, span], sems.at[who * count + j])
            copy.start()
            copies.append(copy)
    finish(copies)


def close(bands, core, parts, rows, cols):
    vmem = pl.BlockSpec(memory_space=pltpu.VMEM)
    flat = [value for part in parts for value in part]
    return pl.pallas_call(
        functools.partial(close_kernel, bands),
        out_shape=jax.ShapeDtypeStruct((2, rows, cols), F32),
        in_specs=[pl.BlockSpec(memory_space=pltpu.SMEM)] + [vmem] * len(flat),
        out_specs=pl.BlockSpec(memory_space=pl.ANY),
        scratch_shapes=[pltpu.VMEM((2, rows, cols), F32), pltpu.SemaphoreType.DMA((2 * len(bands),))],
        compiler_params=pltpu.CompilerParams(vmem_limit_bytes=24 * MIB),
        name="close",
    )(core, *flat)


def per_device(perturb, control, diffusivity, sea_mask, fold_partner):
    rows, cols = diffusivity.shape
    lon_count, lat_count = lax.axis_size("lon"), lax.axis_size("lat")
    lat = lax.axis_index("lat")
    start = fold_partner[0]
    core = (lax.axis_index("mem") % 2).astype(jnp.int32).reshape(1)
    place = jnp.stack([lat.astype(jnp.int32), start % cols])
    swap = functools.partial(lax.ppermute, axis_name="mem", perm=[(i, i ^ 1) for i in range(4)])
    across = functools.partial(lax.ppermute, axis_name="mem", perm=[(i, i ^ 2) for i in range(4)])
    size = rows // 4
    bands = [(i * size, size) for i in range(4)]
    args = (core, control, perturb, diffusivity, sea_mask)

    low, high, message = edges(place, control, diffusivity, sea_mask)
    low_rows = lax.ppermute(message, "lat", [(0, 1), (1, 0)])

    def folded(a):
        def branch(value):
            return tuple(
                lax.ppermute(
                    value,
                    ("lon", "lat"),
                    [((a - n - i) % lon_count * lat_count + 1, i * lat_count + 1) for i in range(lon_count)],
                )
                for n in range(2)
            )

        return branch

    fold_a, fold_b = lax.switch(start // cols, [folded(a) for a in range(lon_count)], high)
    west, east, to_east, to_west, south, north = pack_strips(
        place, control, diffusivity, sea_mask, low_rows, fold_a, fold_b
    )
    from_west = lax.ppermute(to_east, "lon", [(i, (i + 1) % lon_count) for i in range(lon_count)])
    from_east = lax.ppermute(to_west, "lon", [(i, (i - 1) % lon_count) for i in range(lon_count)])
    rim_keep, rim_send = rim_sums(core, west, east, from_west, from_east, low, high, south, north, perturb)

    parts = []
    for j, (at, count) in enumerate(bands):
        last = j == len(bands) - 1
        other = swap(band(False, at, count, *args, rim=rim_send if last else None))
        mine = band(True, at, count, *args, rim=rim_keep if last else None, other=other)
        far = across(mine)
        parts.append((mine, far, swap(mine), swap(far)))
    return close(bands, core, parts, rows, cols)


def solution(mesh):
    return jax.shard_map(
        per_device,
        mesh=mesh,
        in_specs=(
            P("mem", None, "lat", "lon"),
            P("mem", None, "lat", "lon"),
            P("lat", "lon"),
            P(None, "lat", "lon"),
            P(),
        ),
        out_specs=P(None, "lat", "lon"),
        check_vma=False,
    )
```

time: 454 us -> 135 us (0.30)
  the two profiles are of different devices: /device:TPU:1 before, /device:TPU:25 now
where the time goes in v1:
time: 135 us; the launch traced here: 136 us
  Pallas kernels  68.2 us (51%)
  starting transfers between devices  33.2 us (25%)
  waiting for transfers between devices  18.3 us (14%)
  local copies, waits for them, and re-layouts  13 us (10%)
  between operations  2.8 us (2%)
    pallas_call x1, Pallas kernels, rim_sums(): pl.pallas_call(rim_kernel, out_shape=[jax.ShapeDtypeStruct((size, LANES),...  45.4 us
    pallas_call x8, Pallas kernels, band(): pl.pallas_call(functools.partial(band_kernel, keep, low, rows, rim is not...  15.9 us
    unnamed x22, local copies, waits for them, and re-layouts  11.8 us
    ppermute x2, starting transfers between devices, branch(): lax.ppermute(value, ('lon', 'lat'), [((a - n - i) % lon_count * lat_count...  9.95 us
    ppermute x4, waiting for transfers between devices, per_device(): far = across(mine)  8.76 us
    ppermute x8, starting transfers between devices, per_device(): parts.append((mine, far, swap(mine), swap(far)))  7.5 us
    ppermute x2, waiting for transfers between devices, branch(): lax.ppermute(value, ('lon', 'lat'), [((a - n - i) % lon_count * lat_count...  6.3 us
    ppermute x4, starting transfers between devices, per_device(): far = across(mine)  6.1 us
  transfers between devices with their start and end apart: 21, of which 7 were waited for; matrix products, arithmetic and copies ran while one was open for 0% of the time, Pallas kernels for 48%

profile of v1, /device:TPU:25, one launch (start us, length us, event | category | flops | bytes accessed | tf_op | source)
XLA Modules:
  0.0 135.8 jit_solution(11503121384478250565)
XLA Ops:
  0.0 1.2 slice.3
  3.1 2.2 %copy-done = f32[2,2,1024,256]{3,2,1,0:T(8,128)S(1)} copy-done((f32[2,2,1024,256]{3,2,1,0:T(8,128)S(1)}, f32[2,2,1024,256]{3,2,1,0:T(8,128)}, u32[]{:S(2)}) %copy-start) | copy-done | bytes 4194328
  5.3 1.6 %copy-done.6 = s32[2,1024,256]{2,1,0:T(8,128)S(1)} copy-done((s32[2,1024,256]{2,1,0:T(8,128)S(1)}, s32[2,1024,256]{2,1,0:T(8,128)}, u32[]{:S(2)}) %copy-start.6) | copy-done | bytes 2097176
  10.0 2.2 %copy-done.1 = f32[2,2,1024,256]{3,2,1,0:T(8,128)S(1)} copy-done((f32[2,2,1024,256]{3,2,1,0:T(8,128)S(1)}, f32[2,2,1024,256]{3,2,1,0:T(8,128)}, u32[]{:S(2)}) %copy-start.1) | copy-done | bytes 4194328
  12.2 2.2 %copy-done.4 = f32[2,2,1024,256]{3,2,1,0:T(8,128)S(1)} copy-done((f32[2,2,1024,256]{3,2,1,0:T(8,128)S(1)}, f32[2,2,1024,256]{3,2,1,0:T(8,128)}, u32[]{:S(2)}) %copy-start.4) | copy-done | bytes 4194328
  14.4 2.6 %band_send.4 = f32[512,128]{1,0:T(8,128)} custom-call(s32[1]{0:T(128)} %bitcast.core, f32[2,2,1024,256]{3,2,1,0:T(8,128)S(1)} %copy-done.1, f32[2,2,1024,256]{3,2,1,0:T(8,128)S(1)} %copy-done.4, f32[1024,256]{1,0:T(8,128)S(1)} %copy-done.9, s32[2,1024,256]{2,1,0:T(8,128)S(1)} %copy-done.7), custom_call_target="tpu_custom_call" | custom-call | flops 13107200 | bytes 2097152 | tf_op jit(solution)/shard_map/band_send/pallas_call | solution.py:169
  18.5 16.3 %conditional.1 = (f32[7,8,256]{2,1,0:T(8,128)}, f32[7,8,256]{2,1,0:T(8,128)}) conditional(s32[]{:T(128)} %clamp.3, f32[7,8,256]{2,1,0:T(8,128)} %get-tuple-element.35.high, f32[7,8,256]{2,1,0:T(8,128)} %get-tuple-element.35.high, f32[7,8,256]{2,1,0:T(8,128)} %get-tuple-element.35.high, ...), branch_computations={%region_0.1_spmd, %region_1.2_spmd, %region_2.3_spmd, %region_3.4_... | conditional | bytes 458848 | solution.py:529
  18.5 7.7 %collective-permute-start.31 = (f32[7,8,256]{2,1,0:T(8,128)}, f32[7,8,256]{2,1,0:T(8,128)}, u32[]{:S(2)}, u32[]{:S(2)}) collective-permute-start(f32[7,8,256]{2,1,0:T(8,128)} %param.15), channel_id=1, source_target_pairs={{116,4},{108,12},{100,20},{92,28},{84,36},{76,44},{68,52},{60,60},... | collective-permute-start | bytes 172040 | tf_op jit(solution)/shard_map/cond/branch_15_fun/ppermute | solution.py:519
  26.2 2.2 %collective-permute-start.30 = (f32[7,8,256]{2,1,0:T(8,128)}, f32[7,8,256]{2,1,0:T(8,128)}, u32[]{:S(2)}, u32[]{:S(2)}) collective-permute-start(f32[7,8,256]{2,1,0:T(8,128)} %param.15), channel_id=1, source_target_pairs={{124,4},{116,12},{108,20},{100,28},{92,36},{84,44},{76,52},{68,60}... | collective-permute-start | bytes 172040 | tf_op jit(solution)/shard_map/cond/branch_15_fun/ppermute | solution.py:519
  28.8 6.0 %collective-permute-done.30 = f32[7,8,256]{2,1,0:T(8,128)} collective-permute-done((f32[7,8,256]{2,1,0:T(8,128)}, f32[7,8,256]{2,1,0:T(8,128)}, u32[]{:S(2)}, u32[]{:S(2)}) %collective-permute-start.30) | collective-permute-done | bytes 57376 | tf_op jit(solution)/shard_map/cond/branch_15_fun/ppermute | solution.py:519
  34.8 2.2 %copy-done.2 = f32[2,2,1024,256]{3,2,1,0:T(8,128)S(1)} copy-done((f32[2,2,1024,256]{3,2,1,0:T(8,128)S(1)}, f32[2,2,1024,256]{3,2,1,0:T(8,128)}, u32[]{:S(2)}) %copy-start.2) | copy-done | bytes 4194328
  36.9 4.2 %pack_strips.1 = (f32[1040,128]{1,0:T(8,128)S(1)}, f32[1040,128]{1,0:T(8,128)S(1)}, f32[208,128]{1,0:T(8,128)S(1)}, f32[208,128]{1,0:T(8,128)S(1)}, f32[7,8,256]{2,1,0:T(8,128)S(1)}, /*index=5*/f32[7,8,256]{2,1,0:T(8,128)S(1)}) custom-call(s32[2]{0:T(128)S(1)} %pad_add_fusion.place, f32[2,2,1024,256]{3,2,1,0:T(8,128)S(1)} %copy-done.2, ...), custom_call_target="tpu_custom_call" | custom-call | tf_op jit(solution)/shard_map/pack_strips/pallas_call | solution.py:304
  41.3 4.8 %collective-permute-start.46 = (f32[208,128]{1,0:T(8,128)S(1)}, f32[208,128]{1,0:T(8,128)S(1)}, u32[]{:S(2)}, u32[]{:S(2)}) collective-permute-start(f32[208,128]{1,0:T(8,128)S(1)} %get-tuple-element.41), channel_id=1, source_target_pairs={{0,120},{8,0},{16,8},{24,16},{32,24},{40,32},{48,40},{56,48},{64,5... | collective-permute-start | bytes 319496 | tf_op jit(solution)/shard_map/ppermute | solution.py:534
  46.1 2.1 %collective-permute-done.45.from_west = f32[208,128]{1,0:T(8,128)S(1)} collective-permute-done((f32[208,128]{1,0:T(8,128)S(1)}, f32[208,128]{1,0:T(8,128)S(1)}, u32[]{:S(2)}, u32[]{:S(2)}) %collective-permute-start.45) | collective-permute-done | bytes 106528 | tf_op jit(solution)/shard_map/ppermute | solution.py:533
  48.2 45.4 %rim_sums.1 = (f32[80,128]{1,0:T(8,128)S(1)}, f32[80,128]{1,0:T(8,128)S(1)}) custom-call(s32[1]{0:T(128)} %bitcast.core, f32[1040,128]{1,0:T(8,128)S(1)} %get-tuple-element.38.west_in, f32[1040,128]{1,0:T(8,128)S(1)} %get-tuple-element.39.east_in, f32[208,128]{1,0:T(8,128)S(1)} %collective-permute-done.45.from_west, ...), custom_call_target="tpu_custom_call" | custom-call | tf_op jit(solution)/shard_map/rim_sums/pallas_call | solution.py:432
  93.6 1.9 %band_send.7 = f32[592,128]{1,0:T(8,128)S(1)} custom-call(s32[1]{0:T(128)} %bitcast.core, f32[2,2,1024,256]{3,2,1,0:T(8,128)S(1)} %copy-done.3, f32[2,2,1024,256]{3,2,1,0:T(8,128)S(1)} %copy-done.5, f32[1024,256]{1,0:T(8,128)S(1)} %copy-done.9, s32[2,1024,256]{2,1,0:T(8,128)S(1)} %copy-done.7, f32[80,128]{1,0:T(8,128)S(1)} %get-tuple-element.46.rest_0_), custom_call_target="tpu_custom_call" | custom-call | flops 13107200 | bytes 2097152 | tf_op jit(solution)/shard_map/band_send/pallas_call | solution.py:169
  95.5 2.7 %collective-permute-start.47 = (f32[592,128]{1,0:T(8,128)S(1)}, f32[592,128]{1,0:T(8,128)S(1)}, u32[]{:S(2)}, u32[]{:S(2)}) collective-permute-start(f32[592,128]{1,0:T(8,128)S(1)} %band_send.7), channel_id=1, source_target_pairs={{0,1},{1,0},{2,3},{3,2},{4,5},{5,4},{6,7},{7,6},{8,9},{9,8},{10,11... | collective-permute-start | bytes 909320 | tf_op jit(solution)/shard_map/ppermute | solution.py:540
  98.2 1.9 %band_send.5 = f32[512,128]{1,0:T(8,128)S(1)} custom-call(s32[1]{0:T(128)} %bitcast.core, f32[2,2,1024,256]{3,2,1,0:T(8,128)S(1)} %copy-done.3, f32[2,2,1024,256]{3,2,1,0:T(8,128)S(1)} %copy-done.5, f32[1024,256]{1,0:T(8,128)S(1)} %copy-done.9, s32[2,1024,256]{2,1,0:T(8,128)S(1)} %copy-done.7), custom_call_target="tpu_custom_call" | custom-call | flops 13107200 | bytes 2097152 | tf_op jit(solution)/shard_map/band_send/pallas_call | solution.py:169
  100.4 1.9 %band_send.6 = f32[512,128]{1,0:T(8,128)S(1)} custom-call(s32[1]{0:T(128)} %bitcast.core, f32[2,2,1024,256]{3,2,1,0:T(8,128)S(1)} %copy-done.3, f32[2,2,1024,256]{3,2,1,0:T(8,128)S(1)} %copy-done.5, f32[1024,256]{1,0:T(8,128)S(1)} %copy-done.9, s32[2,1024,256]{2,1,0:T(8,128)S(1)} %copy-done.7), custom_call_target="tpu_custom_call" | custom-call | flops 13107200 | bytes 2097152 | tf_op jit(solution)/shard_map/band_send/pallas_call | solution.py:169
  102.9 1.9 %band_keep.4.rest_0_ = f32[512,128]{1,0:T(8,128)S(1)} custom-call(s32[1]{0:T(128)} %bitcast.core, f32[2,2,1024,256]{3,2,1,0:T(8,128)S(1)} %copy-done.3, f32[2,2,1024,256]{3,2,1,0:T(8,128)S(1)} %copy-done.5, f32[1024,256]{1,0:T(8,128)S(1)} %copy-done.9, s32[2,1024,256]{2,1,0:T(8,128)S(1)} %copy-done.7, f32[512,128]{1,0:T(8,128)S(1)} %collective-permute-done.32.rest_0_), custom_call_target="tpu_custom_call" | custom-call | flops 13107200 | bytes 2097152 | tf_op jit(solution)/shard_map/band_keep/pallas_call | solution.py:169
  105.9 1.9 %band_keep.7.rest_12_ = f32[592,128]{1,0:T(8,128)S(1)} custom-call(s32[1]{0:T(128)} %bitcast.core, f32[2,2,1024,256]{3,2,1,0:T(8,128)S(1)} %copy-done.3, f32[2,2,1024,256]{3,2,1,0:T(8,128)S(1)} %copy-done.5, f32[1024,256]{1,0:T(8,128)S(1)} %copy-done.9, s32[2,1024,256]{2,1,0:T(8,128)S(1)} %copy-done.7, f32[80,128]{1,0:T(8,128)S(1)} %get-tuple-element.45.rest_0_, ...), custom_call_target="tpu_custom_call" | custom-call | flops 13107200 | bytes 2097152 | tf_op jit(solution)/shard_map/band_keep/pallas_call | solution.py:169
  107.8 2.1 %collective-permute-start.48 = (f32[592,128]{1,0:T(8,128)S(1)}, f32[592,128]{1,0:T(8,128)S(1)}, u32[]{:S(2)}, u32[]{:S(2)}) collective-permute-start(f32[592,128]{1,0:T(8,128)S(1)} %band_keep.7.rest_12_), channel_id=1, source_target_pairs={{0,2},{1,3},{2,0},{3,1},{4,6},{5,7},{6,4},{7,5},{8,10},{9,11},{10,... | collective-permute-start | bytes 909320 | tf_op jit(solution)/shard_map/ppermute | solution.py:542
  109.9 1.9 %band_keep.5.rest_4_ = f32[512,128]{1,0:T(8,128)S(1)} custom-call(s32[1]{0:T(128)} %bitcast.core, f32[2,2,1024,256]{3,2,1,0:T(8,128)S(1)} %copy-done.3, f32[2,2,1024,256]{3,2,1,0:T(8,128)S(1)} %copy-done.5, f32[1024,256]{1,0:T(8,128)S(1)} %copy-done.9, s32[2,1024,256]{2,1,0:T(8,128)S(1)} %copy-done.7, f32[512,128]{1,0:T(8,128)S(1)} %collective-permute-done.36.rest_0_), custom_call_target="tpu_custom_call" | custom-call | flops 13107200 | bytes 2097152 | tf_op jit(solution)/shard_map/band_keep/pallas_call | solution.py:169
  113.8 1.9 %band_keep.6.rest_8_ = f32[512,128]{1,0:T(8,128)S(1)} custom-call(s32[1]{0:T(128)} %bitcast.core, f32[2,2,1024,256]{3,2,1,0:T(8,128)S(1)} %copy-done.3, f32[2,2,1024,256]{3,2,1,0:T(8,128)S(1)} %copy-done.5, f32[1024,256]{1,0:T(8,128)S(1)} %copy-done.9, s32[2,1024,256]{2,1,0:T(8,128)S(1)} %copy-done.7, f32[512,128]{1,0:T(8,128)S(1)} %collective-permute-done.40.rest_0_), custom_call_target="tpu_custom_call" | custom-call | flops 13107200 | bytes 2097152 | tf_op jit(solution)/shard_map/band_keep/pallas_call | solution.py:169
  116.2 2.1 %collective-permute-start.41 = (f32[512,128]{1,0:T(8,128)S(1)}, f32[512,128]{1,0:T(8,128)S(1)}, u32[]{:S(2)}, u32[]{:S(2)}) collective-permute-start(f32[512,128]{1,0:T(8,128)S(1)} %band_keep.6.rest_8_), channel_id=1, source_target_pairs={{0,2},{1,3},{2,0},{3,1},{4,6},{5,7},{6,4},{7,5},{8,10},{9,11},{10,... | collective-permute-start | bytes 786440 | tf_op jit(solution)/shard_map/ppermute | solution.py:542
  118.7 1.7 %collective-permute-done.48.rest_13_ = f32[592,128]{1,0:T(8,128)S(1)} collective-permute-done((f32[592,128]{1,0:T(8,128)S(1)}, f32[592,128]{1,0:T(8,128)S(1)}, u32[]{:S(2)}, u32[]{:S(2)}) %collective-permute-start.48) | collective-permute-done | bytes 303136 | tf_op jit(solution)/shard_map/ppermute | solution.py:542
  120.4 2.1 %collective-permute-start.50 = (f32[592,128]{1,0:T(8,128)S(1)}, f32[592,128]{1,0:T(8,128)S(1)}, u32[]{:S(2)}, u32[]{:S(2)}) collective-permute-start(f32[592,128]{1,0:T(8,128)S(1)} %collective-permute-done.48.rest_13_), channel_id=1, source_target_pairs={{0,1},{1,0},{2,3},{3,2},{4,5},{5,4},{6,7},{7,6},{8,9},{9,8},{10,11... | collective-permute-start | bytes 909320 | tf_op jit(solution)/shard_map/ppermute | solution.py:543
  122.5 3.5 %collective-permute-done.37.rest_5_ = f32[512,128]{1,0:T(8,128)S(1)} collective-permute-done((f32[512,128]{1,0:T(8,128)S(1)}, f32[512,128]{1,0:T(8,128)S(1)}, u32[]{:S(2)}, u32[]{:S(2)}) %collective-permute-start.37) | collective-permute-done | bytes 262176 | tf_op jit(solution)/shard_map/ppermute | solution.py:542
  126.0 2.1 %collective-permute-start.35 = (f32[512,128]{1,0:T(8,128)S(1)}, f32[512,128]{1,0:T(8,128)S(1)}, u32[]{:S(2)}, u32[]{:S(2)}) collective-permute-start(f32[512,128]{1,0:T(8,128)S(1)} %collective-permute-done.33.rest_1_), channel_id=1, source_target_pairs={{0,1},{1,0},{2,3},{3,2},{4,5},{5,4},{6,7},{7,6},{8,9},{9,8},{10,11... | collective-permute-start | bytes 786440 | tf_op jit(solution)/shard_map/ppermute | solution.py:543
  128.1 3.5 %collective-permute-done.41.rest_9_ = f32[512,128]{1,0:T(8,128)S(1)} collective-permute-done((f32[512,128]{1,0:T(8,128)S(1)}, f32[512,128]{1,0:T(8,128)S(1)}, u32[]{:S(2)}, u32[]{:S(2)}) %collective-permute-start.41) | collective-permute-done | bytes 262176 | tf_op jit(solution)/shard_map/ppermute | solution.py:542
  131.7 1.3 collective-permute-start.43
  134.1 1.5 %close.1 = f32[2,1024,256]{2,1,0:T(8,128)} custom-call(s32[1]{0:T(128)} %bitcast.core, f32[512,128]{1,0:T(8,128)S(1)} %band_keep.4.rest_0_, f32[512,128]{1,0:T(8,128)S(1)} %collective-permute-done.33.rest_1_, f32[512,128]{1,0:T(8,128)S(1)} %collective-permute-done.34.rest_2_, f32[512,128]{1,0:T(8,128)S(1)} %collective-permute-done.35.rest_3_, ...), custom_call_target="tpu_custom_call" | custom-call | tf_op jit(solution)/shard_map/close/pallas_call | solution.py:489
  (47 shorter events, 10.4 us)
Async XLA Ops:
  3.1 2.2 %copy-start = (f32[2,2,1024,256]{3,2,1,0:T(8,128)S(1)}, f32[2,2,1024,256]{3,2,1,0:T(8,128)}, u32[]{:S(2)}) copy-start(f32[2,2,1024,256]{3,2,1,0:T(8,128)} %control.17) | copy-start | bytes 12582916
  5.3 1.6 %copy-start.6 = (s32[2,1024,256]{2,1,0:T(8,128)S(1)}, s32[2,1024,256]{2,1,0:T(8,128)}, u32[]{:S(2)}) copy-start(s32[2,1024,256]{2,1,0:T(8,128)} %mask.17) | copy-start | bytes 6291460
  6.9 1.2 copy-start.8
  8.1 1.7 %copy-start.7 = (s32[2,1024,256]{2,1,0:T(8,128)S(1)}, s32[2,1024,256]{2,1,0:T(8,128)}, u32[]{:S(2)}) copy-start(s32[2,1024,256]{2,1,0:T(8,128)} %mask.17) | copy-start | bytes 6291460
  8.1 1.9 %copy-start.9 = (f32[1024,256]{1,0:T(8,128)S(1)}, f32[1024,256]{1,0:T(8,128)}, u32[]{:S(2)}) copy-start(f32[1024,256]{1,0:T(8,128)} %kappa.17) | copy-start | bytes 3145732
  9.3 25.4 %collective-permute-start.44 = (f32[7,8,256]{2,1,0:T(8,128)}, f32[7,8,256]{2,1,0:T(8,128)S(1)}, u32[]{:S(2)}, u32[]{:S(2)}) collective-permute-start(f32[7,8,256]{2,1,0:T(8,128)} %get-tuple-element.34), channel_id=1, source_target_pairs={{0,4},{4,0},{1,5},{5,1},{2,6},{6,2},{3,7},{7,3},{8,12},{12,8},{9,1... | collective-permute-start | bytes 172040 | tf_op jit(solution)/shard_map/ppermute | solution.py:514
  10.0 2.2 %copy-start.1 = (f32[2,2,1024,256]{3,2,1,0:T(8,128)S(1)}, f32[2,2,1024,256]{3,2,1,0:T(8,128)}, u32[]{:S(2)}) copy-start(f32[2,2,1024,256]{3,2,1,0:T(8,128)} %control.17) | copy-start | bytes 12582916
  12.2 2.2 %copy-start.4 = (f32[2,2,1024,256]{3,2,1,0:T(8,128)S(1)}, f32[2,2,1024,256]{3,2,1,0:T(8,128)}, u32[]{:S(2)}) copy-start(f32[2,2,1024,256]{3,2,1,0:T(8,128)} %perturb.17) | copy-start | bytes 12582916
  17.0 85.9 %collective-permute-start.32 = (f32[512,128]{1,0:T(8,128)}, f32[512,128]{1,0:T(8,128)S(1)}, u32[]{:S(2)}, u32[]{:S(2)}) collective-permute-start(f32[512,128]{1,0:T(8,128)} %band_send.4), channel_id=1, source_target_pairs={{0,1},{1,0},{2,3},{3,2},{4,5},{5,4},{6,7},{7,6},{8,9},{9,8},{10,11... | collective-permute-start | bytes 786440 | tf_op jit(solution)/shard_map/ppermute | solution.py:540
  18.5 10.3 %collective-permute-start.31 = (f32[7,8,256]{2,1,0:T(8,128)}, f32[7,8,256]{2,1,0:T(8,128)}, u32[]{:S(2)}, u32[]{:S(2)}) collective-permute-start(f32[7,8,256]{2,1,0:T(8,128)} %param.15), channel_id=1, source_target_pairs={{116,4},{108,12},{100,20},{92,28},{84,36},{76,44},{68,52},{60,60},... | collective-permute-start | bytes 172040 | tf_op jit(solution)/shard_map/cond/branch_15_fun/ppermute | solution.py:519
  26.2 8.6 %collective-permute-start.30 = (f32[7,8,256]{2,1,0:T(8,128)}, f32[7,8,256]{2,1,0:T(8,128)}, u32[]{:S(2)}, u32[]{:S(2)}) collective-permute-start(f32[7,8,256]{2,1,0:T(8,128)} %param.15), channel_id=1, source_target_pairs={{124,4},{116,12},{108,20},{100,28},{92,36},{84,44},{76,52},{68,60}... | collective-permute-start | bytes 172040 | tf_op jit(solution)/shard_map/cond/branch_15_fun/ppermute | solution.py:519
  34.8 2.2 %copy-start.2 = (f32[2,2,1024,256]{3,2,1,0:T(8,128)S(1)}, f32[2,2,1024,256]{3,2,1,0:T(8,128)}, u32[]{:S(2)}) copy-start(f32[2,2,1024,256]{3,2,1,0:T(8,128)} %control.17) | copy-start | bytes 12582916
  36.9 11.2 %copy-start.5 = (f32[2,2,1024,256]{3,2,1,0:T(8,128)S(1)}, f32[2,2,1024,256]{3,2,1,0:T(8,128)}, u32[]{:S(2)}) copy-start(f32[2,2,1024,256]{3,2,1,0:T(8,128)} %perturb.17) | copy-start | bytes 12582916
  36.9 11.2 %copy-start.10 = (f32[7,8,256]{2,1,0:T(8,128)S(1)}, f32[7,8,256]{2,1,0:T(8,128)}, u32[]{:S(2)}) copy-start(f32[7,8,256]{2,1,0:T(8,128)} %get-tuple-element.35.high) | copy-start | bytes 172036
  41.2 52.4 %copy-start.3 = (f32[2,2,1024,256]{3,2,1,0:T(8,128)S(1)}, f32[2,2,1024,256]{3,2,1,0:T(8,128)}, u32[]{:S(2)}) copy-start(f32[2,2,1024,256]{3,2,1,0:T(8,128)} %control.17) | copy-start | bytes 12582916
  41.2 6.9 %collective-permute-start.45 = (f32[208,128]{1,0:T(8,128)S(1)}, f32[208,128]{1,0:T(8,128)S(1)}, u32[]{:S(2)}, u32[]{:S(2)}) collective-permute-start(f32[208,128]{1,0:T(8,128)S(1)} %get-tuple-element.40), channel_id=1, source_target_pairs={{0,8},{8,16},{16,24},{24,32},{32,40},{40,48},{48,56},{56,64},{64,7... | collective-permute-start | bytes 319496 | tf_op jit(solution)/shard_map/ppermute | solution.py:533
  41.3 6.9 %collective-permute-start.46 = (f32[208,128]{1,0:T(8,128)S(1)}, f32[208,128]{1,0:T(8,128)S(1)}, u32[]{:S(2)}, u32[]{:S(2)}) collective-permute-start(f32[208,128]{1,0:T(8,128)S(1)} %get-tuple-element.41), channel_id=1, source_target_pairs={{0,120},{8,0},{16,8},{24,16},{32,24},{40,32},{48,40},{56,48},{64,5... | collective-permute-start | bytes 319496 | tf_op jit(solution)/shard_map/ppermute | solution.py:534
  95.5 10.3 %collective-permute-start.47 = (f32[592,128]{1,0:T(8,128)S(1)}, f32[592,128]{1,0:T(8,128)S(1)}, u32[]{:S(2)}, u32[]{:S(2)}) collective-permute-start(f32[592,128]{1,0:T(8,128)S(1)} %band_send.7), channel_id=1, source_target_pairs={{0,1},{1,0},{2,3},{3,2},{4,5},{5,4},{6,7},{7,6},{8,9},{9,8},{10,11... | collective-permute-start | bytes 909320 | tf_op jit(solution)/shard_map/ppermute | solution.py:540
  100.1 9.8 %collective-permute-start.36 = (f32[512,128]{1,0:T(8,128)S(1)}, f32[512,128]{1,0:T(8,128)S(1)}, u32[]{:S(2)}, u32[]{:S(2)}) collective-permute-start(f32[512,128]{1,0:T(8,128)S(1)} %band_send.5), channel_id=1, source_target_pairs={{0,1},{1,0},{2,3},{3,2},{4,5},{5,4},{6,7},{7,6},{8,9},{9,8},{10,11... | collective-permute-start | bytes 786440 | tf_op jit(solution)/shard_map/ppermute | solution.py:540
  102.3 10.6 %collective-permute-start.40 = (f32[512,128]{1,0:T(8,128)S(1)}, f32[512,128]{1,0:T(8,128)S(1)}, u32[]{:S(2)}, u32[]{:S(2)}) collective-permute-start(f32[512,128]{1,0:T(8,128)S(1)} %band_send.6), channel_id=1, source_target_pairs={{0,1},{1,0},{2,3},{3,2},{4,5},{5,4},{6,7},{7,6},{8,9},{9,8},{10,11... | collective-permute-start | bytes 786440 | tf_op jit(solution)/shard_map/ppermute | solution.py:540
  104.8 10.9 %collective-permute-start.34 = (f32[512,128]{1,0:T(8,128)S(1)}, f32[512,128]{1,0:T(8,128)S(1)}, u32[]{:S(2)}, u32[]{:S(2)}) collective-permute-start(f32[512,128]{1,0:T(8,128)S(1)} %band_keep.4.rest_0_), channel_id=1, source_target_pairs={{0,1},{1,0},{2,3},{3,2},{4,5},{5,4},{6,7},{7,6},{8,9},{9,8},{10,11... | collective-permute-start | bytes 786440 | tf_op jit(solution)/shard_map/ppermute | solution.py:543
  104.9 11.3 %collective-permute-start.33 = (f32[512,128]{1,0:T(8,128)S(1)}, f32[512,128]{1,0:T(8,128)S(1)}, u32[]{:S(2)}, u32[]{:S(2)}) collective-permute-start(f32[512,128]{1,0:T(8,128)S(1)} %band_keep.4.rest_0_), channel_id=1, source_target_pairs={{0,2},{1,3},{2,0},{3,1},{4,6},{5,7},{6,4},{7,5},{8,10},{9,11},{10,... | collective-permute-start | bytes 786440 | tf_op jit(solution)/shard_map/ppermute | solution.py:542
  107.8 12.7 %collective-permute-start.48 = (f32[592,128]{1,0:T(8,128)S(1)}, f32[592,128]{1,0:T(8,128)S(1)}, u32[]{:S(2)}, u32[]{:S(2)}) collective-permute-start(f32[592,128]{1,0:T(8,128)S(1)} %band_keep.7.rest_12_), channel_id=1, source_target_pairs={{0,2},{1,3},{2,0},{3,1},{4,6},{5,7},{6,4},{7,5},{8,10},{9,11},{10,... | collective-permute-start | bytes 909320 | tf_op jit(solution)/shard_map/ppermute | solution.py:542
  111.8 6.4 %collective-permute-start.38 = (f32[512,128]{1,0:T(8,128)S(1)}, f32[512,128]{1,0:T(8,128)S(1)}, u32[]{:S(2)}, u32[]{:S(2)}) collective-permute-start(f32[512,128]{1,0:T(8,128)S(1)} %band_keep.5.rest_4_), channel_id=1, source_target_pairs={{0,1},{1,0},{2,3},{3,2},{4,5},{5,4},{6,7},{7,6},{8,9},{9,8},{10,11... | collective-permute-start | bytes 786440 | tf_op jit(solution)/shard_map/ppermute | solution.py:543
  112.9 13.2 %collective-permute-start.37 = (f32[512,128]{1,0:T(8,128)S(1)}, f32[512,128]{1,0:T(8,128)S(1)}, u32[]{:S(2)}, u32[]{:S(2)}) collective-permute-start(f32[512,128]{1,0:T(8,128)S(1)} %band_keep.5.rest_4_), channel_id=1, source_target_pairs={{0,2},{1,3},{2,0},{3,1},{4,6},{5,7},{6,4},{7,5},{8,10},{9,11},{10,... | collective-permute-start | bytes 786440 | tf_op jit(solution)/shard_map/ppermute | solution.py:542
  115.7 12.4 %collective-permute-start.42 = (f32[512,128]{1,0:T(8,128)S(1)}, f32[512,128]{1,0:T(8,128)S(1)}, u32[]{:S(2)}, u32[]{:S(2)}) collective-permute-start(f32[512,128]{1,0:T(8,128)S(1)} %band_keep.6.rest_8_), channel_id=1, source_target_pairs={{0,1},{1,0},{2,3},{3,2},{4,5},{5,4},{6,7},{7,6},{8,9},{9,8},{10,11... | collective-permute-start | bytes 786440 | tf_op jit(solution)/shard_map/ppermute | solution.py:543
  116.2 15.5 %collective-permute-start.41 = (f32[512,128]{1,0:T(8,128)S(1)}, f32[512,128]{1,0:T(8,128)S(1)}, u32[]{:S(2)}, u32[]{:S(2)}) collective-permute-start(f32[512,128]{1,0:T(8,128)S(1)} %band_keep.6.rest_8_), channel_id=1, source_target_pairs={{0,2},{1,3},{2,0},{3,1},{4,6},{5,7},{6,4},{7,5},{8,10},{9,11},{10,... | collective-permute-start | bytes 786440 | tf_op jit(solution)/shard_map/ppermute | solution.py:542
  118.2 14.7 %collective-permute-start.49 = (f32[592,128]{1,0:T(8,128)S(1)}, f32[592,128]{1,0:T(8,128)S(1)}, u32[]{:S(2)}, u32[]{:S(2)}) collective-permute-start(f32[592,128]{1,0:T(8,128)S(1)} %band_keep.7.rest_12_), channel_id=1, source_target_pairs={{0,1},{1,0},{2,3},{3,2},{4,5},{5,4},{6,7},{7,6},{8,9},{9,8},{10,11... | collective-permute-start | bytes 909320 | tf_op jit(solution)/shard_map/ppermute | solution.py:543
  120.4 13.7 %collective-permute-start.50 = (f32[592,128]{1,0:T(8,128)S(1)}, f32[592,128]{1,0:T(8,128)S(1)}, u32[]{:S(2)}, u32[]{:S(2)}) collective-permute-start(f32[592,128]{1,0:T(8,128)S(1)} %collective-permute-done.48.rest_13_), channel_id=1, source_target_pairs={{0,1},{1,0},{2,3},{3,2},{4,5},{5,4},{6,7},{7,6},{8,9},{9,8},{10,11... | collective-permute-start | bytes 909320 | tf_op jit(solution)/shard_map/ppermute | solution.py:543
  126.0 6.9 %collective-permute-start.35 = (f32[512,128]{1,0:T(8,128)S(1)}, f32[512,128]{1,0:T(8,128)S(1)}, u32[]{:S(2)}, u32[]{:S(2)}) collective-permute-start(f32[512,128]{1,0:T(8,128)S(1)} %collective-permute-done.33.rest_1_), channel_id=1, source_target_pairs={{0,1},{1,0},{2,3},{3,2},{4,5},{5,4},{6,7},{7,6},{8,9},{9,8},{10,11... | collective-permute-start | bytes 786440 | tf_op jit(solution)/shard_map/ppermute | solution.py:543
  128.1 4.8 %collective-permute-start.39 = (f32[512,128]{1,0:T(8,128)S(1)}, f32[512,128]{1,0:T(8,128)S(1)}, u32[]{:S(2)}, u32[]{:S(2)}) collective-permute-start(f32[512,128]{1,0:T(8,128)S(1)} %collective-permute-done.37.rest_5_), channel_id=1, source_target_pairs={{0,1},{1,0},{2,3},{3,2},{4,5},{5,4},{6,7},{7,6},{8,9},{9,8},{10,11... | collective-permute-start | bytes 786440 | tf_op jit(solution)/shard_map/ppermute | solution.py:543
  131.7 2.4 %collective-permute-start.43 = (f32[512,128]{1,0:T(8,128)S(1)}, f32[512,128]{1,0:T(8,128)S(1)}, u32[]{:S(2)}, u32[]{:S(2)}) collective-permute-start(f32[512,128]{1,0:T(8,128)S(1)} %collective-permute-done.41.rest_9_), channel_id=1, source_target_pairs={{0,1},{1,0},{2,3},{3,2},{4,5},{5,4},{6,7},{7,6},{8,9},{9,8},{10,11... | collective-permute-start | bytes 786440 | tf_op jit(solution)/shard_map/ppermute | solution.py:543
